TPU v7x, 32 devices: a whole 2x2x4 slice. The times are simulated.
32 devices in a mesh: shard: 8 (over z, y), tensor: 4 (over x, core).
Axes of the slice: x: 2, y: 2, z: 4, core: 2. Of those that a mesh axis runs over, the one named last changes fastest.
Arguments:
- attn_weight: float32 [4, 2048, 2048], P(None, 'shard', 'tensor'), may hold values from -62 to 62
- ffin_weight: float32 [2, 2048, 5120], P(None, 'shard', 'tensor'), may hold values from -62 to 62
- ffout_weight: float32 [1, 5120, 2048], P(None, 'shard', 'tensor'), may hold values from -62 to 62
- attn_grad: float32 [4, 2048, 2048], P(None, 'shard', 'tensor'), may hold values from -62 to 62
- ffin_grad: float32 [2, 2048, 5120], P(None, 'shard', 'tensor'), may hold values from -62 to 62
- ffout_grad: float32 [1, 5120, 2048], P(None, 'shard', 'tensor'), may hold values from -62 to 62
- attn_first: float32 [4, 2048, 2048], P(None, ('shard', 'tensor')), may hold values from -62 to 62
- ffin_first: float32 [2, 5120, 2048], P(None, ('shard', 'tensor')), may hold values from -62 to 62
- ffout_first: float32 [1, 2048, 5120], P(None, ('shard', 'tensor')), may hold values from -62 to 62
- attn_second: float32 [4, 2048, 2048], P(None, ('shard', 'tensor')), may hold values from 0.01 to 1
- ffin_second: float32 [2, 5120, 2048], P(None, ('shard', 'tensor')), may hold values from 0.01 to 1
- ffout_second: float32 [1, 2048, 5120], P(None, ('shard', 'tensor')), may hold values from 0.01 to 1
Outputs:
- attn_new: float32 [4, 2048, 2048], P(None, 'shard', 'tensor')
- ffin_new: float32 [2, 2048, 5120], P(None, 'shard', 'tensor')
- ffout_new: float32 [1, 5120, 2048], P(None, 'shard', 'tensor')
- attn_first_new: float32 [4, 2048, 2048], P(None, ('shard', 'tensor'))
- ffin_first_new: float32 [2, 5120, 2048], P(None, ('shard', 'tensor'))
- ffout_first_new: float32 [1, 2048, 5120], P(None, ('shard', 'tensor'))
- attn_second_new: float32 [4, 2048, 2048], P(None, ('shard', 'tensor'))
- ffin_second_new: float32 [2, 5120, 2048], P(None, ('shard', 'tensor'))
- ffout_second_new: float32 [1, 2048, 5120], P(None, ('shard', 'tensor'))
- trust_ratio: float32 [7], replicated
All inputs are finite; a program needn't handle non-finite values.
Results may differ from a plain program's by a relative error of at most 0.00002.
Values sent between devices are 32-bit elements; how exact they have to be, the bound alone decides.
A program may use at most 128 MiB of HBM per device.

v0:
```python
import jax
import jax.numpy as jnp
from jax import lax
from jax.sharding import PartitionSpec as P

beta_one = 0.9
beta_two = 0.999
step_number = 10.0
correct_one = 1.0 - beta_one**step_number
correct_two = 1.0 - beta_two**step_number
learn_rate = 0.02
decay_rate = 0.1
epsilon = 1e-06


def moment_step(gradient_t, first_moment, second):
    first_new = beta_one * first_moment + (1.0 - beta_one) * gradient_t
    second_new = beta_two * second + (1.0 - beta_two) * gradient_t * gradient_t
    ratio_value = first_new / correct_one / (jnp.sqrt(second_new / correct_two) + epsilon)
    return (first_new, second_new, ratio_value)


def outbound(block, shard_count, tensor_count):
    stacks, row_block, col_block = block.shape
    groups = shard_count // tensor_count
    col_flat = col_block // shard_count
    turned = jnp.swapaxes(block, 1, 2)
    return turned.reshape(stacks, groups, tensor_count, col_flat * row_block)


def arrived_flat(piece, row_block):
    stacks, shard_count, single, length = piece.shape
    col_flat = length // row_block
    spread = piece.reshape(stacks, shard_count, col_flat, row_block)
    return jnp.transpose(spread, (0, 2, 1, 3)).reshape(stacks, col_flat, shard_count * row_block)


def homebound(flat, row_block):
    stacks, col_flat, rows_all = flat.shape
    shard_count = rows_all // row_block
    spread = flat.reshape(stacks, col_flat, shard_count, row_block)
    return jnp.transpose(spread, (0, 2, 1, 3)).reshape(stacks, shard_count, 1, col_flat * row_block)


def arrived_block(piece, row_block):
    stacks, groups, tensor_count, length = piece.shape
    col_flat = length // row_block
    spread = piece.reshape(stacks, groups * tensor_count * col_flat, row_block)
    return jnp.swapaxes(spread, 1, 2)


def shards(
    attn_weight,
    ffin_weight,
    ffout_weight,
    attn_grad,
    ffin_grad,
    ffout_grad,
    attn_first,
    ffin_first,
    ffout_first,
    attn_second,
    ffin_second,
    ffout_second,
):
    shard_count = lax.axis_size("shard")
    tensor_count = lax.axis_size("tensor")
    weights = (attn_weight, ffin_weight, ffout_weight)
    firsts = (attn_first, ffin_first, ffout_first)
    seconds = (attn_second, ffin_second, ffout_second)
    row_blocks = [matrix.shape[1] for matrix in weights]
    weight_sq = jnp.concatenate([jnp.sum(matrix * matrix, axis=(1, 2)) for matrix in weights])
    weight_total = lax.psum(weight_sq, ("shard", "tensor"))
    arrived = (
        lax.all_to_all(
            lax.all_to_all(
                outbound(attn_grad, shard_count, tensor_count),
                "tensor",
                split_axis=2,
                concat_axis=1,
                tiled=True,
            ),
            "shard",
            split_axis=1,
            concat_axis=1,
            tiled=True,
        ),
        lax.all_to_all(
            lax.all_to_all(
                outbound(ffin_grad, shard_count, tensor_count),
                "tensor",
                split_axis=2,
                concat_axis=1,
                tiled=True,
            ),
            "shard",
            split_axis=1,
            concat_axis=1,
            tiled=True,
        ),
        lax.all_to_all(
            lax.all_to_all(
                outbound(ffout_grad, shard_count, tensor_count),
                "tensor",
                split_axis=2,
                concat_axis=1,
                tiled=True,
            ),
            "shard",
            split_axis=1,
            concat_axis=1,
            tiled=True,
        ),
        lax.all_to_all(
            lax.all_to_all(
                outbound(attn_weight, shard_count, tensor_count),
                "tensor",
                split_axis=2,
                concat_axis=1,
                tiled=True,
            ),
            "shard",
            split_axis=1,
            concat_axis=1,
            tiled=True,
        ),
        lax.all_to_all(
            lax.all_to_all(
                outbound(ffin_weight, shard_count, tensor_count),
                "tensor",
                split_axis=2,
                concat_axis=1,
                tiled=True,
            ),
            "shard",
            split_axis=1,
            concat_axis=1,
            tiled=True,
        ),
        lax.all_to_all(
            lax.all_to_all(
                outbound(ffout_weight, shard_count, tensor_count),
                "tensor",
                split_axis=2,
                concat_axis=1,
                tiled=True,
            ),
            "shard",
            split_axis=1,
            concat_axis=1,
            tiled=True,
        ),
    )
    flat_grads = [arrived_flat(arrived[position], row_blocks[position]) for position in range(3)]
    flat_weights = [
        arrived_flat(arrived[position + 3], row_blocks[position]) for position in range(3)
    ]
    results = [
        moment_step(flat_grads[position], firsts[position], seconds[position])
        for position in range(3)
    ]
    updates = [results[position][2] + decay_rate * flat_weights[position] for position in range(3)]
    update_sq = jnp.concatenate([jnp.sum(member * member, axis=(1, 2)) for member in updates])
    update_total = lax.psum(update_sq, ("shard", "tensor"))
    trust_ratio = jnp.sqrt(weight_total) / (jnp.sqrt(update_total) + epsilon)
    scales = (trust_ratio[0:4], trust_ratio[4:6], trust_ratio[6:7])
    stepped = [
        flat_weights[position] - learn_rate * scales[position][:, None, None] * updates[position]
        for position in range(3)
    ]
    restored = (
        lax.all_to_all(
            lax.all_to_all(
                homebound(stepped[0], row_blocks[0]),
                "shard",
                split_axis=1,
                concat_axis=1,
                tiled=True,
            ),
            "tensor",
            split_axis=1,
            concat_axis=2,
            tiled=True,
        ),
        lax.all_to_all(
            lax.all_to_all(
                homebound(stepped[1], row_blocks[1]),
                "shard",
                split_axis=1,
                concat_axis=1,
                tiled=True,
            ),
            "tensor",
            split_axis=1,
            concat_axis=2,
            tiled=True,
        ),
        lax.all_to_all(
            lax.all_to_all(
                homebound(stepped[2], row_blocks[2]),
                "shard",
                split_axis=1,
                concat_axis=1,
                tiled=True,
            ),
            "tensor",
            split_axis=1,
            concat_axis=2,
            tiled=True,
        ),
    )
    new_weights = [arrived_block(restored[position], row_blocks[position]) for position in range(3)]
    return (
        new_weights[0],
        new_weights[1],
        new_weights[2],
        results[0][0],
        results[1][0],
        results[2][0],
        results[0][1],
        results[1][1],
        results[2][1],
        trust_ratio,
    )


def solution(mesh):
    in_specs = (
        P(None, "shard", "tensor"),
        P(None, "shard", "tensor"),
        P(None, "shard", "tensor"),
        P(None, "shard", "tensor"),
        P(None, "shard", "tensor"),
        P(None, "shard", "tensor"),
        P(None, ("shard", "tensor"), None),
        P(None, ("shard", "tensor"), None),
        P(None, ("shard", "tensor"), None),
        P(None, ("shard", "tensor"), None),
        P(None, ("shard", "tensor"), None),
        P(None, ("shard", "tensor"), None),
    )
    out_specs = (
        P(None, "shard", "tensor"),
        P(None, "shard", "tensor"),
        P(None, "shard", "tensor"),
        P(None, ("shard", "tensor"), None),
        P(None, ("shard", "tensor"), None),
        P(None, ("shard", "tensor"), None),
        P(None, ("shard", "tensor"), None),
        P(None, ("shard", "tensor"), None),
        P(None, ("shard", "tensor"), None),
        P(),
    )
    return jax.shard_map(shards, mesh=mesh, in_specs=in_specs, out_specs=out_specs, check_vma=False)
```

profile of v0, /device:TPU:0, one launch (start us, length us, event | category | flops | bytes accessed | tf_op | source)
XLA Modules:
  0.0 794.6 jit_solution(17819097669537399784)
XLA Ops:
  5.0 4.2 all-to-all-start.8
  14.7 11.8 %all-to-all-done.8 = f32[1,2,4,40960]{3,1,0,2:T(2,128)S(1)} async-done(((f32[1,2,4,40960]{3,1,0,2:T(2,128)}), f32[1,2,4,40960]{3,1,0,2:T(2,128)S(1)}, u32[]{:S(2)}, u32[]{:S(2)}) %all-to-all-start.8) | async-done | bytes 1310752 | tf_op jit(solution)/shard_map/all_to_all | solution.py:102
  26.5 4.3 all-to-all-start.10
  39.0 9.2 %all-to-all-done.10 = f32[1,2,4,40960]{3,1,0,2:T(2,128)} async-done(((f32[1,2,4,40960]{3,1,0,2:T(2,128)}), f32[1,2,4,40960]{3,1,0,2:T(2,128)}, u32[]{:S(2)}, u32[]{:S(2)}) %all-to-all-start.10) | async-done | bytes 1310752 | tf_op jit(solution)/shard_map/all_to_all | solution.py:141
  48.2 4.5 all-to-all-start.2
  59.7 18.7 %all-to-all-done.2 = f32[4,2,4,16384]{3,1,0,2:T(2,128)} async-done(((f32[4,2,4,16384]{3,1,0,2:T(2,128)}), f32[4,2,4,16384]{3,1,0,2:T(2,128)}, u32[]{:S(2)}, u32[]{:S(2)}) %all-to-all-start.2) | async-done | bytes 2097184 | tf_op jit(solution)/shard_map/all_to_all | solution.py:76
  78.4 4.9 all-to-all-start
  91.6 17.5 %all-to-all-done = f32[4,2,4,16384]{3,1,0,2:T(2,128)} async-done(((f32[4,2,4,16384]{3,1,0,2:T(2,128)}), f32[4,2,4,16384]{3,1,0,2:T(2,128)}, u32[]{:S(2)}, u32[]{:S(2)}) %all-to-all-start) | async-done | bytes 2097184 | tf_op jit(solution)/shard_map/all_to_all | solution.py:115
  109.0 4.5 all-to-all-start.4
  119.4 5.3 copy.97
  124.6 20.3 %all-to-all-done.4 = f32[2,2,4,40960]{3,1,0,2:T(2,128)} async-done(((f32[2,2,4,40960]{3,1,0,2:T(2,128)}), f32[2,2,4,40960]{3,1,0,2:T(2,128)}, u32[]{:S(2)}, u32[]{:S(2)}) %all-to-all-start.4) | async-done | bytes 2621472 | tf_op jit(solution)/shard_map/all_to_all | solution.py:89
  145.0 4.6 all-to-all-start.6
  149.6 4.4 all_to_all.161
  154.0 26.9 %all-to-all-done.6 = f32[2,2,4,40960]{3,1,0,2:T(2,128)} async-done(((f32[2,2,4,40960]{3,1,0,2:T(2,128)}), f32[2,2,4,40960]{3,1,0,2:T(2,128)}, u32[]{:S(2)}, u32[]{:S(2)}) %all-to-all-start.6) | async-done | bytes 2621472 | tf_op jit(solution)/shard_map/all_to_all | solution.py:128
  180.9 6.6 all-to-all-start.9
  187.5 4.4 all_to_all.166
  192.0 26.9 %all-to-all-done.9 = f32[1,8,1,40960]{3,2,0,1:T(1,128)} async-done(((f32[1,8,1,40960]{3,2,0,1:T(1,128)}), f32[1,8,1,40960]{3,2,0,1:T(1,128)}, u32[]{:S(2)}, u32[]{:S(2)}) %all-to-all-start.9) | async-done | bytes 1310752 | tf_op jit(solution)/shard_map/all_to_all | solution.py:101
  218.8 4.3 all-to-all-start.11
  223.1 4.3 copy.86
  227.4 26.8 %all-to-all-done.11 = f32[1,8,1,40960]{3,2,0,1:T(1,128)} async-done(((f32[1,8,1,40960]{3,2,0,1:T(1,128)}), f32[1,8,1,40960]{3,2,0,1:T(1,128)}, u32[]{:S(2)}, u32[]{:S(2)}) %all-to-all-start.11) | async-done | bytes 1310752 | tf_op jit(solution)/shard_map/all_to_all | solution.py:140
  254.2 4.4 all-to-all-start.3
  258.5 4.3 copy.80
  262.8 43.5 %all-to-all-done.3 = f32[4,8,1,16384]{3,0,2,1:T(4,128)} async-done(((f32[4,8,1,16384]{3,0,2,1:T(4,128)}), f32[4,8,1,16384]{3,0,2,1:T(4,128)}, u32[]{:S(2)}, u32[]{:S(2)}) %all-to-all-start.3) | async-done | bytes 2097184 | tf_op jit(solution)/shard_map/all_to_all | solution.py:75
  306.3 4.5 all-to-all-start.1
  310.8 5.3 copy.92
  316.0 42.6 %all-to-all-done.1 = f32[4,8,1,16384]{3,0,2,1:T(4,128)} async-done(((f32[4,8,1,16384]{3,0,2,1:T(4,128)}), f32[4,8,1,16384]{3,0,2,1:T(4,128)}, u32[]{:S(2)}, u32[]{:S(2)}) %all-to-all-start.1) | async-done | bytes 2097184 | tf_op jit(solution)/shard_map/all_to_all | solution.py:114
  358.6 4.4 all-to-all-start.5
  363.0 5.3 copy.98
  368.3 53.7 %all-to-all-done.5 = f32[2,8,1,40960]{3,0,2,1:T(2,128)} async-done(((f32[2,8,1,40960]{3,0,2,1:T(2,128)}), f32[2,8,1,40960]{3,0,2,1:T(2,128)}, u32[]{:S(2)}, u32[]{:S(2)}) %all-to-all-start.5) | async-done | bytes 2621472 | tf_op jit(solution)/shard_map/all_to_all | solution.py:88
  422.0 4.4 all-to-all-start.7
  431.0 4.4 reduce.2
  435.8 4.4 reduce.3
  467.4 18.0 %all-to-all-done.7 = f32[2,8,1,40960]{3,0,2,1:T(2,128)} async-done(((f32[2,8,1,40960]{3,0,2,1:T(2,128)}), f32[2,8,1,40960]{3,0,2,1:T(2,128)}, u32[]{:S(2)}, u32[]{:S(2)}) %all-to-all-start.7) | async-done | bytes 2621472 | tf_op jit(solution)/shard_map/all_to_all | solution.py:127
  485.4 4.9 reshape.193
  493.6 6.0 multiply_reduce_fusion
  501.0 37.6 %all-reduce = (f32[7]{0:T(128)S(1)}, f32[7]{0:T(128)S(1)}) all-reduce(f32[7]{0:T(128)S(1)} %get-tuple-element.52, f32[7]{0:T(128)S(1)} %get-tuple-element.51), channel_id=1, replica_groups=mesh['shard'=8,'tensor'=4] {'shard','tensor'}, use_global_device_ids=true, to_apply=%region_7.0 | all-reduce | flops 14 | bytes 112 | tf_op jit(solution)/shard_map/psum | solution.py:164
  547.0 35.9 %all_to_all.198 = f32[1,8,1,40960]{3,2,0,1:T(1,128)} all-to-all(f32[1,8,1,40960]{3,2,0,1:T(1,128)} %reshape.194), channel_id=1, replica_groups=mesh['shard'=8,'tensor'=4] {'shard'}, dimensions={1} | all-to-all | bytes 2621440 | tf_op jit(solution)/shard_map/all_to_all | solution.py:199
  582.9 4.7 all-to-all-start.17
  587.6 4.0 multiply_subtract_fusion.1
  595.9 4.3 copy.111
  600.2 4.7 all-to-all-done.17
  604.9 4.4 all-to-all-start.12
  609.4 3.9 multiply_subtract_fusion
  619.1 38.5 %all-to-all-done.12 = f32[4,8,1,16384]{3,0,2,1:T(4,128)} async-done(((f32[4,8,1,16384]{3,0,2,1:T(4,128)}), f32[4,8,1,16384]{3,0,2,1:T(4,128)}, u32[]{:S(2)}, u32[]{:S(2)}) %all-to-all-start.12) | async-done | bytes 2097184 | tf_op jit(solution)/shard_map/all_to_all | solution.py:173
  657.6 63.1 %all_to_all.199 = f32[2,8,1,40960]{3,0,2,1:T(2,128)} all-to-all(f32[2,8,1,40960]{3,0,2,1:T(2,128)S(1)} %copy.114), channel_id=1, replica_groups=mesh['shard'=8,'tensor'=4] {'shard'}, dimensions={1} | all-to-all | bytes 5242880 | tf_op jit(solution)/shard_map/all_to_all | solution.py:186
  720.7 30.1 %all_to_all.200 = f32[4,8,1,16384]{3,0,2,1:T(4,128)} all-to-all(f32[4,8,1,16384]{3,0,2,1:T(4,128)} %all-to-all-done.12), channel_id=1, replica_groups=mesh['shard'=8,'tensor'=4] {'tensor'}, dimensions={1} | all-to-all | bytes 4194304 | tf_op jit(solution)/shard_map/all_to_all | solution.py:172
  764.0 4.3 copy.152
  774.8 11.2 %all-to-all-done.15 = f32[2,8,1,40960]{3,0,2,1:T(2,128)S(1)} async-done(((f32[2,8,1,40960]{3,0,2,1:T(2,128)}), f32[2,8,1,40960]{3,0,2,1:T(2,128)S(1)}, u32[]{:S(2)}, u32[]{:S(2)}) %all-to-all-start.15) | async-done | bytes 2621472 | tf_op jit(solution)/shard_map/all_to_all | solution.py:185
  (83 shorter events, 121.6 us)
Async XLA Ops:
  2.9 6.3 copy-start.5
  5.0 21.5 %all-to-all-start.8 = ((f32[1,2,4,40960]{3,1,0,2:T(2,128)}), f32[1,2,4,40960]{3,1,0,2:T(2,128)S(1)}, u32[]{:S(2)}, u32[]{:S(2)}) async-start(f32[1,2,4,40960]{3,1,0,2:T(2,128)} %copy.103), calls=%async_computation.8 | async-start | bytes 2621440 | tf_op jit(solution)/shard_map/all_to_all | solution.py:102
  26.5 4.3 copy-start.6
  26.5 21.7 %all-to-all-start.10 = ((f32[1,2,4,40960]{3,1,0,2:T(2,128)}), f32[1,2,4,40960]{3,1,0,2:T(2,128)}, u32[]{:S(2)}, u32[]{:S(2)}) async-start(f32[1,2,4,40960]{3,1,0,2:T(2,128)} %copy.107), calls=%async_computation.10 | async-start | bytes 2621440 | tf_op jit(solution)/shard_map/all_to_all | solution.py:141
  39.0 13.7 %copy-start.4 = (f32[4,256,512]{2,1,0:T(8,128)S(1)}, f32[4,256,512]{2,1,0:T(8,128)}, u32[]{:S(2)}) copy-start(f32[4,256,512]{2,1,0:T(8,128)} %param.12) | copy-start | bytes 6291460
  48.2 30.2 %all-to-all-start.2 = ((f32[4,2,4,16384]{3,1,0,2:T(2,128)}), f32[4,2,4,16384]{3,1,0,2:T(2,128)}, u32[]{:S(2)}, u32[]{:S(2)}) async-start(f32[4,2,4,16384]{3,1,0,2:T(2,128)} %copy.85), calls=%async_computation.2 | async-start | bytes 4194304 | tf_op jit(solution)/shard_map/all_to_all | solution.py:76
  59.7 23.6 %copy-start.7 = (f32[2,256,1280]{2,1,0:T(8,128)S(1)}, f32[2,256,1280]{2,1,0:T(8,128)}, u32[]{:S(2)}) copy-start(f32[2,256,1280]{2,1,0:T(8,128)} %param.16) | copy-start | bytes 7864324
  78.4 30.7 %all-to-all-start = ((f32[4,2,4,16384]{3,1,0,2:T(2,128)}), f32[4,2,4,16384]{3,1,0,2:T(2,128)}, u32[]{:S(2)}, u32[]{:S(2)}) async-start(f32[4,2,4,16384]{3,1,0,2:T(2,128)} %copy.79), calls=%async_computation | async-start | bytes 4194304 | tf_op jit(solution)/shard_map/all_to_all | solution.py:115
  91.6 22.0 %copy-start.2 = (f32[2,256,1280]{2,1,0:T(8,128)S(1)}, f32[2,256,1280]{2,1,0:T(8,128)}, u32[]{:S(2)}) copy-start(f32[2,256,1280]{2,1,0:T(8,128)} %param.13) | copy-start | bytes 7864324
  109.0 35.9 %all-to-all-start.4 = ((f32[2,2,4,40960]{3,1,0,2:T(2,128)}), f32[2,2,4,40960]{3,1,0,2:T(2,128)}, u32[]{:S(2)}, u32[]{:S(2)}) async-start(f32[2,2,4,40960]{3,1,0,2:T(2,128)} %copy.91), calls=%async_computation.4 | async-start | bytes 5242880 | tf_op jit(solution)/shard_map/all_to_all | solution.py:89
  145.0 36.0 %all-to-all-start.6 = ((f32[2,2,4,40960]{3,1,0,2:T(2,128)}), f32[2,2,4,40960]{3,1,0,2:T(2,128)}, u32[]{:S(2)}, u32[]{:S(2)}) async-start(f32[2,2,4,40960]{3,1,0,2:T(2,128)} %copy.97), calls=%async_computation.6 | async-start | bytes 5242880 | tf_op jit(solution)/shard_map/all_to_all | solution.py:128
  180.9 37.9 %all-to-all-start.9 = ((f32[1,8,1,40960]{3,2,0,1:T(1,128)}), f32[1,8,1,40960]{3,2,0,1:T(1,128)}, u32[]{:S(2)}, u32[]{:S(2)}) async-start(f32[1,8,1,40960]{3,2,0,1:T(1,128)} %bitcast.167), calls=%async_computation.9 | async-start | bytes 2621440 | tf_op jit(solution)/shard_map/all_to_all | solution.py:101
  218.8 35.3 %all-to-all-start.11 = ((f32[1,8,1,40960]{3,2,0,1:T(1,128)}), f32[1,8,1,40960]{3,2,0,1:T(1,128)}, u32[]{:S(2)}, u32[]{:S(2)}) async-start(f32[1,8,1,40960]{3,2,0,1:T(1,128)} %bitcast.168), calls=%async_computation.11 | async-start | bytes 2621440 | tf_op jit(solution)/shard_map/all_to_all | solution.py:140
  254.2 52.1 %all-to-all-start.3 = ((f32[4,8,1,16384]{3,0,2,1:T(4,128)}), f32[4,8,1,16384]{3,0,2,1:T(4,128)}, u32[]{:S(2)}, u32[]{:S(2)}) async-start(f32[4,8,1,16384]{3,0,2,1:T(4,128)} %bitcast.156), calls=%async_computation.3 | async-start | bytes 4194304 | tf_op jit(solution)/shard_map/all_to_all | solution.py:75
  306.3 52.3 %all-to-all-start.1 = ((f32[4,8,1,16384]{3,0,2,1:T(4,128)}), f32[4,8,1,16384]{3,0,2,1:T(4,128)}, u32[]{:S(2)}, u32[]{:S(2)}) async-start(f32[4,8,1,16384]{3,0,2,1:T(4,128)} %bitcast.157), calls=%async_computation.1 | async-start | bytes 4194304 | tf_op jit(solution)/shard_map/all_to_all | solution.py:114
  358.6 63.4 %all-to-all-start.5 = ((f32[2,8,1,40960]{3,0,2,1:T(2,128)}), f32[2,8,1,40960]{3,0,2,1:T(2,128)}, u32[]{:S(2)}, u32[]{:S(2)}) async-start(f32[2,8,1,40960]{3,0,2,1:T(2,128)} %bitcast.146), calls=%async_computation.5 | async-start | bytes 5242880 | tf_op jit(solution)/shard_map/all_to_all | solution.py:88
  422.0 63.4 %all-to-all-start.7 = ((f32[2,8,1,40960]{3,0,2,1:T(2,128)}), f32[2,8,1,40960]{3,0,2,1:T(2,128)}, u32[]{:S(2)}, u32[]{:S(2)}) async-start(f32[2,8,1,40960]{3,0,2,1:T(2,128)} %bitcast.144), calls=%async_computation.7 | async-start | bytes 5242880 | tf_op jit(solution)/shard_map/all_to_all | solution.py:127
  440.2 1.4 copy-start.11
  440.2 2.2 copy-start.12
  440.6 1.1 copy-start.1
  454.8 3.4 copy-start.9
  454.8 3.4 copy-start.10
  456.9 1.3 copy-start
  490.3 2.5 copy-start.3
  490.3 3.3 copy-start.8
  538.6 70.7 %copy-start.13 = (f32[7]{0:T(128)}, f32[7]{0:T(128)S(1)}, u32[]{:S(2)}) copy-start(f32[7]{0:T(128)S(1)} %add_divide_fusion) | copy-start | bytes 88
  582.9 22.0 %all-to-all-start.17 = ((f32[1,8,1,40960]{3,2,0,1:T(1,128)}), f32[1,8,1,40960]{3,2,0,1:T(1,128)}, u32[]{:S(2)}, u32[]{:S(2)}) async-start(f32[1,8,1,40960]{3,2,0,1:T(1,128)} %all_to_all.198), calls=%async_computation.17 | async-start | bytes 2621440 | tf_op jit(solution)/shard_map/all_to_all | solution.py:198
  604.9 52.7 %all-to-all-start.12 = ((f32[4,8,1,16384]{3,0,2,1:T(4,128)}), f32[4,8,1,16384]{3,0,2,1:T(4,128)}, u32[]{:S(2)}, u32[]{:S(2)}) async-start(f32[4,8,1,16384]{3,0,2,1:T(4,128)} %copy.111), calls=%async_computation.12 | async-start | bytes 4194304 | tf_op jit(solution)/shard_map/all_to_all | solution.py:173
  750.9 35.1 %all-to-all-start.15 = ((f32[2,8,1,40960]{3,0,2,1:T(2,128)}), f32[2,8,1,40960]{3,0,2,1:T(2,128)S(1)}, u32[]{:S(2)}, u32[]{:S(2)}) async-start(f32[2,8,1,40960]{3,0,2,1:T(2,128)} %all_to_all.199), calls=%async_computation.15 | async-start | bytes 5242880 | tf_op jit(solution)/shard_map/all_to_all | solution.py:185
where the time goes:
time: 804 us; the launch traced here: 795 us
  waiting for transfers between devices  370 us (46%)
  blocking collectives  167 us (21%)
  local copies, waits for them, and re-layouts  149 us (19%)
  starting transfers between devices  68.5 us (9%)
  other arithmetic  38.2 us (5%)
    all_to_all x1, blocking collectives, shards(): lax.all_to_all(homebound(stepped[1], row_blocks[1]), 'shard', split_axis=...  63.1 us
    all_to_all x1, waiting for transfers between devices, shards(): lax.all_to_all(lax.all_to_all(outbound(ffin_grad, shard_count, tensor_cou...  53.7 us
    all_to_all x1, waiting for transfers between devices, shards(): lax.all_to_all(lax.all_to_all(outbound(attn_grad, shard_count, tensor_cou...  43.5 us
    all_to_all x1, waiting for transfers between devices, shards(): lax.all_to_all(lax.all_to_all(outbound(attn_weight, shard_count, tensor_c...  42.6 us
    all_to_all x1, waiting for transfers between devices, shards(): lax.all_to_all(homebound(stepped[0], row_blocks[0]), 'shard', split_axis=...  38.5 us
    psum x1, blocking collectives, shards(): update_total = lax.psum(update_sq, ('shard', 'tensor'))  37.6 us
    all_to_all x1, blocking collectives, shards(): lax.all_to_all(homebound(stepped[2], row_blocks[2]), 'shard', split_axis=...  35.9 us
    reshape x12, local copies, waits for them, and re-layouts, outbound(): return turned.reshape(stacks, groups, tensor_count, col_flat * row_block)  32.2 us
  transfers between devices with their start and end apart: 15, of which 15 were waited for; matrix products, arithmetic and copies ran while one was open for 17% of the time, Pallas kernels for 0%

commit v1 on v0

v1 whole, which is shorter than its diff:
```python
import functools

import jax
import jax.numpy as jnp
from jax import lax
from jax.experimental import pallas as pl
from jax.experimental.pallas import tpu as pltpu
from jax.sharding import PartitionSpec as P

MESH = pl.DeviceIdType.MESH
RELAY_OUT = False
RELAY_BACK = False

beta_one = 0.9
beta_two = 0.999
step_number = 10.0
correct_one = 1.0 - beta_one**step_number
correct_two = 1.0 - beta_two**step_number
learn_rate = 0.02
decay_rate = 0.1
epsilon = 1e-06


def moment_step(gradient_t, first_moment, second):
    first_new = beta_one * first_moment + (1.0 - beta_one) * gradient_t
    second_new = beta_two * second + (1.0 - beta_two) * gradient_t * gradient_t
    ratio_value = first_new / correct_one / (jnp.sqrt(second_new / correct_two) + epsilon)
    return (first_new, second_new, ratio_value)


def outbound(block, shard_count, tensor_count):
    stacks, row_block, col_block = block.shape
    groups = shard_count // tensor_count
    col_flat = col_block // shard_count
    turned = jnp.swapaxes(block, 1, 2)
    return turned.reshape(stacks, groups, tensor_count, col_flat * row_block)


def arrived_flat(piece, row_block):
    stacks, shard_count, single, length = piece.shape
    col_flat = length // row_block
    spread = piece.reshape(stacks, shard_count, col_flat, row_block)
    return jnp.transpose(spread, (0, 2, 1, 3)).reshape(stacks, col_flat, shard_count * row_block)


def homebound(flat, row_block):
    stacks, col_flat, rows_all = flat.shape
    shard_count = rows_all // row_block
    spread = flat.reshape(stacks, col_flat, shard_count, row_block)
    return jnp.transpose(spread, (0, 2, 1, 3)).reshape(stacks, shard_count, 1, col_flat * row_block)


def arrived_block(piece, row_block):
    stacks, groups, tensor_count, length = piece.shape
    col_flat = length // row_block
    spread = piece.reshape(stacks, groups * tensor_count * col_flat, row_block)
    return jnp.swapaxes(spread, 1, 2)


ORDER = ((1, 0), (1, 1), (2, 0), (0, 0), (0, 1), (0, 2), (0, 3))


def row_of(array, index):
    return (0, 4, 6)[array] + index


def exchange_kernel(shard_count, tensor_count, *refs):
    weights, grads, firsts, seconds = refs[0:3], refs[3:6], refs[6:9], refs[9:12]
    updates, firsts_new, seconds_new, sums_out = refs[12:15], refs[15:18], refs[18:21], refs[21]
    grad_v, turned_v, flat_v, back_v = refs[22:25], refs[25:28], refs[28:31], refs[31:34]
    first_v, second_v, weight_v = refs[34:37], refs[37:40], refs[40:43]
    out_stop, back_stop = refs[43:46], refs[46:49]
    partial, sums_v = refs[49], refs[50]
    (
        load_g, load_m, load_v, load_w, out_send, out_recv, stop_recv, stop_send,
        back_send, back_recv, bstop_recv, bstop_send, save_u, save_m, save_v, total_sem,
    ) = refs[51:67]

    groups = shard_count // tensor_count
    half = tensor_count // 2
    devices = shard_count * tensor_count
    s, t = lax.axis_index("shard"), lax.axis_index("tensor")
    me = s * tensor_count + t
    mate = lax.rem(t + half, tensor_count)
    side = t // half
    home = s // groups
    mine = lax.rem(s, groups) * tensor_count + t
    my_slot = lax.rem(s, groups) * half + lax.rem(t, half)
    same_side = home // half == side

    for position, (a, i) in enumerate(ORDER):
        pltpu.make_async_copy(grads[a].at[i], grad_v[a].at[i], load_g.at[position]).start()
    for position, (a, i) in enumerate(ORDER):
        pltpu.make_async_copy(firsts[a].at[i], first_v[a].at[i], load_m.at[position]).start()
        pltpu.make_async_copy(seconds[a].at[i], second_v[a].at[i], load_v.at[position]).start()
        pltpu.make_async_copy(weights[a].at[i], weight_v[a].at[i], load_w.at[position]).start()

    barrier = pltpu.get_barrier_semaphore()

    def greet(step, carry):
        other = lax.rem(me + step, devices)
        pl.semaphore_signal(
            barrier,
            inc=1,
            device_id=(other // tensor_count, lax.rem(other, tensor_count)),
            device_id_type=MESH,
        )
        return carry

    lax.fori_loop(1, devices, greet, 0)

    def sizes(a):
        row_block, col_block = weights[a].shape[1:]
        return row_block, col_block, col_block // shard_count

    def remote(src, dst, send, recv, device):
        return pltpu.make_async_remote_copy(
            src_ref=src, dst_ref=dst, send_sem=send, recv_sem=recv,
            device_id=device, device_id_type=MESH,
        )

    def send_or_keep(is_me, src, dst, send, recv, device):
        @pl.when(is_me)
        def _():
            pltpu.make_async_copy(src, dst, recv).start()

        @pl.when(jnp.logical_not(is_me))
        def _():
            remote(src, dst, send, recv, device).start()

    def wait_bytes(ref, sem):
        pltpu.make_async_copy(ref, ref, sem).wait()

    def turn(position):
        a, i = ORDER[position]
        row_block, col_block, col_flat = sizes(a)
        wait_bytes(grad_v[a].at[i], load_g.at[position])

        def one(j, carry):
            span = pl.ds(pl.multiple_of(j * 128, 128), 128)
            turned_v[a][i, span, :] = grad_v[a][i, :, span].T
            return carry

        lax.fori_loop(0, col_block // 128, one, 0)

    def send_out(position):
        a, i = ORDER[position]
        row_block, col_block, col_flat = sizes(a)
        land = pl.ds(pl.multiple_of(s * row_block, 128), row_block)
        send, recv = out_send.at[position], out_recv.at[position]
        if RELAY_OUT:
            other_side = mate // half
            for y in range(groups):
                rows = pl.ds(
                    pl.multiple_of((y * tensor_count + other_side * half) * col_flat, 8),
                    half * col_flat,
                )
                remote(
                    turned_v[a].at[i, rows, :],
                    out_stop[a].at[i, pl.ds(y * half * col_flat, half * col_flat), :],
                    send,
                    stop_recv.at[position],
                    (s, mate),
                ).start()
            for y in range(groups):
                for core in range(half):
                    target = side * half + core
                    k = y * tensor_count + target
                    rows = pl.ds(pl.multiple_of(k * col_flat, 8), col_flat)
                    shard_to = groups * t + y
                    send_or_keep(
                        jnp.logical_and(shard_to == s, target == t),
                        turned_v[a].at[i, rows, :],
                        flat_v[a].at[i, :, land],
                        send,
                        recv,
                        (shard_to, target),
                    )
        else:
            for k in range(shard_count):
                shard_to, target = groups * t + k // tensor_count, k % tensor_count
                send_or_keep(
                    jnp.logical_and(shard_to == s, target == t),
                    turned_v[a].at[i, pl.ds(k * col_flat, col_flat), :],
                    flat_v[a].at[i, :, land],
                    send,
                    recv,
                    (shard_to, target),
                )

    def forward_out(position):
        if not RELAY_OUT:
            return
        a, i = ORDER[position]
        row_block, col_block, col_flat = sizes(a)
        wait_bytes(out_stop[a].at[i], stop_recv.at[position])
        land = pl.ds(pl.multiple_of(s * row_block, 128), row_block)
        for y in range(groups):
            for core in range(half):
                target = side * half + core
                shard_to = groups * mate + y
                send_or_keep(
                    jnp.logical_and(shard_to == s, target == t),
                    out_stop[a].at[i, pl.ds((y * half + core) * col_flat, col_flat), :],
                    flat_v[a].at[i, :, land],
                    stop_send.at[position],
                    out_recv.at[position],
                    (shard_to, target),
                )

    def moments(position):
        a, i = ORDER[position]
        row_block, col_block, col_flat = sizes(a)
        wait_bytes(flat_v[a].at[i], out_recv.at[position])
        wait_bytes(first_v[a].at[i], load_m.at[position])
        wait_bytes(second_v[a].at[i], load_v.at[position])
        length = shard_count * row_block
        width = 1024 if length % 1024 == 0 else row_block

        def one(j, carry):
            rows = pl.ds(pl.multiple_of(j * 8, 8), 8)
            for at in range(0, length, width):
                cols = pl.ds(at, width)
                first_new, second_new, ratio = moment_step(
                    flat_v[a][i, rows, cols], first_v[a][i, rows, cols], second_v[a][i, rows, cols]
                )
                first_v[a][i, rows, cols] = first_new
                second_v[a][i, rows, cols] = second_new
                flat_v[a][i, rows, cols] = ratio
            return carry

        lax.fori_loop(0, col_flat // 8, one, 0)
        rows = pl.ds(pl.multiple_of(mine * col_flat, 8), col_flat)
        slot = pl.ds(pl.multiple_of(my_slot * col_flat, 8), col_flat)
        for shard_to in range(shard_count):
            piece = flat_v[a].at[i, :, pl.ds(shard_to * row_block, row_block)]

            def direct():
                send_or_keep(
                    jnp.logical_and(s == shard_to, home == t),
                    piece,
                    back_v[a].at[i, rows, :],
                    back_send.at[position],
                    back_recv.at[position],
                    (shard_to, home),
                )

            def by_stop():
                stop = lax.rem(home + half, tensor_count)
                send_or_keep(
                    jnp.logical_and(s == shard_to, stop == t),
                    piece,
                    back_stop[a].at[i, slot, :],
                    back_send.at[position],
                    bstop_recv.at[position],
                    (shard_to, stop),
                )

            if RELAY_BACK:
                pl.when(same_side)(direct)
                pl.when(jnp.logical_not(same_side))(by_stop)
            else:
                direct()
        pltpu.make_async_copy(first_v[a].at[i], firsts_new[a].at[i], save_m.at[position]).start()
        pltpu.make_async_copy(second_v[a].at[i], seconds_new[a].at[i], save_v.at[position]).start()

    def forward_back(position):
        if not RELAY_BACK:
            return
        a, i = ORDER[position]
        row_block, col_block, col_flat = sizes(a)
        wait_bytes(back_stop[a].at[i], bstop_recv.at[position])
        for y in range(groups):
            rows = pl.ds(
                pl.multiple_of((y * tensor_count + side * half) * col_flat, 8), half * col_flat
            )
            remote(
                back_stop[a].at[i, pl.ds(y * half * col_flat, half * col_flat), :],
                back_v[a].at[i, rows, :],
                bstop_send.at[position],
                back_recv.at[position],
                (s, mate),
            ).start()

    def renew(position):
        a, i = ORDER[position]
        row_block, col_block, col_flat = sizes(a)
        wait_bytes(back_v[a].at[i], back_recv.at[position])
        wait_bytes(weight_v[a].at[i], load_w.at[position])

        def fold(block):
            return jnp.sum((block * block).reshape(row_block // 8, 8, 128), axis=0)

        def one(j, carry):
            span = pl.ds(pl.multiple_of(j * 128, 128), 128)
            weight = weight_v[a][i, :, span]
            update = back_v[a][i, span, :].T + decay_rate * weight
            grad_v[a][i, :, span] = update
            return carry[0] + fold(weight), carry[1] + fold(update)

        zero = jnp.zeros((8, 128), jnp.float32)
        weight_sq, update_sq = lax.fori_loop(0, col_block // 128, one, (zero, zero))
        row = row_of(a, i)
        partial[me, row : row + 1, :] = jnp.sum(weight_sq, axis=0, keepdims=True)
        partial[me, row + 8 : row + 9, :] = jnp.sum(update_sq, axis=0, keepdims=True)
        pltpu.make_async_copy(grad_v[a].at[i], updates[a].at[i], save_u.at[position]).start()

    count = len(ORDER)
    partial[me, :, :] = jnp.zeros((16, 128), jnp.float32)
    turn(0)
    pl.semaphore_wait(barrier, devices - 1)
    send_out(0)
    for position in range(1, count):
        turn(position)
        send_out(position)
    forward_out(0)
    for position in range(count):
        if position + 1 < count:
            forward_out(position + 1)
        moments(position)
        if position >= 2:
            forward_back(position - 2)
    renew(0)
    forward_back(count - 2)
    renew(1)
    forward_back(count - 1)
    for position in range(2, count):
        renew(position)

    def tell(step, carry):
        other = lax.rem(me + step, devices)
        remote(
            partial.at[me],
            partial.at[me],
            total_sem.at[0],
            total_sem.at[1],
            (other // tensor_count, lax.rem(other, tensor_count)),
        ).start()
        return carry

    lax.fori_loop(1, devices, tell, 0)
    wait_bytes(partial.at[pl.ds(0, devices - 1)], total_sem.at[1])
    total = lax.fori_loop(
        0, devices, lambda d, sofar: sofar + partial[d], jnp.zeros((16, 128), jnp.float32)
    )
    sums_v[...] = total
    pltpu.make_async_copy(sums_v, sums_out, total_sem.at[2]).start()
    wait_bytes(partial.at[pl.ds(0, devices - 1)], total_sem.at[0])

    out_self = home == t if RELAY_OUT else home == t
    stop_self = home == mate
    back_self = home == t
    if RELAY_BACK:
        back_self = jnp.logical_or(home == t, lax.rem(home + half, tensor_count) == t)

    def wait_less(is_less, ref, i, total_rows, piece_rows, sem):
        @pl.when(is_less)
        def _():
            wait_bytes(ref.at[i, pl.ds(0, total_rows - piece_rows), :], sem)

        @pl.when(jnp.logical_not(is_less))
        def _():
            wait_bytes(ref.at[i], sem)

    for position, (a, i) in enumerate(ORDER):
        row_block, col_block, col_flat = sizes(a)
        wait_less(out_self, turned_v[a], i, col_block, col_flat, out_send.at[position])
        wait_less(back_self, turned_v[a], i, col_block, col_flat, back_send.at[position])
        if RELAY_OUT:
            wait_less(stop_self, out_stop[a], i, col_block // 2, col_flat, stop_send.at[position])
        if RELAY_BACK:
            wait_bytes(back_stop[a].at[i], bstop_send.at[position])
        wait_bytes(grad_v[a].at[i], save_u.at[position])
        wait_bytes(first_v[a].at[i], save_m.at[position])
        wait_bytes(second_v[a].at[i], save_v.at[position])
    wait_bytes(sums_v, total_sem.at[2])


def exchange(weights, grads, firsts, seconds, shard_count, tensor_count):
    f32 = jnp.float32
    blocks = [matrix.shape for matrix in weights]
    flats = [matrix.shape for matrix in firsts]
    turned = [(n, c, r) for n, r, c in blocks]
    halves = [(n, c // 2, r) for n, r, c in blocks]
    devices = shard_count * tensor_count
    shapes = blocks + flats + flats + [(16, 128)]
    scratch = []
    for group in (blocks, turned, flats, turned, flats, flats, blocks, halves, halves):
        scratch += [pltpu.VMEM(shape, f32) for shape in group]
    scratch += [pltpu.VMEM((devices, 16, 128), f32), pltpu.VMEM((16, 128), f32)]
    scratch += [pltpu.SemaphoreType.DMA((len(ORDER),))] * 15 + [pltpu.SemaphoreType.DMA((3,))]
    anywhere = pl.BlockSpec(memory_space=pl.ANY)
    return pl.pallas_call(
        functools.partial(exchange_kernel, shard_count, tensor_count),
        out_shape=[jax.ShapeDtypeStruct(shape, f32) for shape in shapes],
        in_specs=[anywhere] * 12,
        out_specs=[anywhere] * 10,
        scratch_shapes=scratch,
        compiler_params=pltpu.CompilerParams(
            collective_id=0, has_side_effects=True, vmem_limit_bytes=56 * 1024 * 1024
        ),
        name="exchange",
    )(*weights, *grads, *firsts, *seconds)


def fits(weights, firsts, shard_count, tensor_count):
    if shard_count % tensor_count or tensor_count % 2:
        return False
    return all(
        matrix.shape[1] % 128 == 0
        and matrix.shape[2] % 128 == 0
        and matrix.shape[2] % (8 * shard_count) == 0
        for matrix in weights
    )


def shards(*arrays):
    shard_count = lax.axis_size("shard")
    tensor_count = lax.axis_size("tensor")
    weights, grads, firsts, seconds = arrays[0:3], arrays[3:6], arrays[6:9], arrays[9:12]
    if not fits(weights, firsts, shard_count, tensor_count):
        return plain(weights, grads, firsts, seconds, shard_count, tensor_count)
    out = exchange(weights, grads, firsts, seconds, shard_count, tensor_count)
    updates, firsts_new, seconds_new, sums = out[0:3], out[3:6], out[6:9], out[9]
    totals = jnp.sum(sums, axis=1)
    trust_ratio = jnp.sqrt(totals[0:7]) / (jnp.sqrt(totals[8:15]) + epsilon)
    return finish(weights, updates, firsts_new, seconds_new, trust_ratio)


def finish(weights, updates, firsts_new, seconds_new, trust_ratio):
    scales = (trust_ratio[0:4], trust_ratio[4:6], trust_ratio[6:7])
    new_weights = [
        weights[position] - learn_rate * scales[position][:, None, None] * updates[position]
        for position in range(3)
    ]
    return (*new_weights, *firsts_new, *seconds_new, trust_ratio)


def plain(weights, grads, firsts, seconds, shard_count, tensor_count):
    row_blocks = [matrix.shape[1] for matrix in weights]
    results = []
    updates = []
    for position in range(3):
        piece = lax.all_to_all(
            lax.all_to_all(
                outbound(grads[position], shard_count, tensor_count),
                "tensor", split_axis=2, concat_axis=1, tiled=True,
            ),
            "shard", split_axis=1, concat_axis=1, tiled=True,
        )
        flat = arrived_flat(piece, row_blocks[position])
        results.append(moment_step(flat, firsts[position], seconds[position]))
        restored = lax.all_to_all(
            lax.all_to_all(
                homebound(results[position][2], row_blocks[position]),
                "shard", split_axis=1, concat_axis=1, tiled=True,
            ),
            "tensor", split_axis=1, concat_axis=2, tiled=True,
        )
        ratio = arrived_block(restored, row_blocks[position])
        updates.append(ratio + decay_rate * weights[position])
    weight_sq = jnp.concatenate([jnp.sum(member * member, axis=(1, 2)) for member in weights])
    update_sq = jnp.concatenate([jnp.sum(member * member, axis=(1, 2)) for member in updates])
    weight_total, update_total = lax.psum((weight_sq, update_sq), ("shard", "tensor"))
    trust_ratio = jnp.sqrt(weight_total) / (jnp.sqrt(update_total) + epsilon)
    return finish(
        weights, updates, [r[0] for r in results], [r[1] for r in results], trust_ratio
    )


def solution(mesh):
    in_specs = (
        P(None, "shard", "tensor"),
        P(None, "shard", "tensor"),
        P(None, "shard", "tensor"),
        P(None, "shard", "tensor"),
        P(None, "shard", "tensor"),
        P(None, "shard", "tensor"),
        P(None, ("shard", "tensor"), None),
        P(None, ("shard", "tensor"), None),
        P(None, ("shard", "tensor"), None),
        P(None, ("shard", "tensor"), None),
        P(None, ("shard", "tensor"), None),
        P(None, ("shard", "tensor"), None),
    )
    out_specs = (
        P(None, "shard", "tensor"),
        P(None, "shard", "tensor"),
        P(None, "shard", "tensor"),
        P(None, ("shard", "tensor"), None),
        P(None, ("shard", "tensor"), None),
        P(None, ("shard", "tensor"), None),
        P(None, ("shard", "tensor"), None),
        P(None, ("shard", "tensor"), None),
        P(None, ("shard", "tensor"), None),
        P(),
    )
    return jax.shard_map(shards, mesh=mesh, in_specs=in_specs, out_specs=out_specs, check_vma=False)
```

time: 804 us -> 431 us (0.54); the launches traced: 795 us -> 431 us
  Pallas kernels: 0 us -> 406 us
  waiting for transfers between devices: 370 us -> 0 us
  blocking collectives: 167 us -> 0 us
  local copies, waits for them, and re-layouts: 149 us -> 13.2 us
  starting transfers between devices: 68.5 us -> 0 us
  other arithmetic: 38.2 us -> 9.79 us
    pallas_call x0 -> x1, Pallas kernels: none -> 406 us  [exchange(): pl.pallas_call(functools.partial(exchange_kernel, shard_count, tensor_cou...]
    all_to_all x15 -> x0, waiting for transfers between devices: 370 us -> none  [the longest x1 53.7 us: shards(): lax.all_to_all(lax.all_to_all(outbound(ffin_grad, shard_count, tensor_cou...]
    all_to_all x3 -> x0, blocking collectives: 129 us -> none  [the longest x1 63.1 us: shards(): lax.all_to_all(homebound(stepped[1], row_blocks[1]), 'shard', split_axis=...]
    reshape x33 -> x0, local copies, waits for them, and re-layouts: 85.3 us -> none  [the longest x12 32.2 us: outbound(): return turned.reshape(stacks, groups, tensor_count, col_flat * row_block)]
    all_to_all x15 -> x0, starting transfers between devices: 68.5 us -> none  [the longest x1 6.59 us: shards(): lax.all_to_all(lax.all_to_all(outbound(ffout_grad, shard_count, tensor_co...]
    all_to_all x9 -> x0, local copies, waits for them, and re-layouts: 38.5 us -> none  [the longest x1 5.25 us: shards(): lax.all_to_all(outbound(ffin_weight, shard_count, tensor_count), 'tensor'...]
    psum x1 -> x0, blocking collectives: 37.6 us -> none  [shards(): update_total = lax.psum(update_sq, ('shard', 'tensor'))]
    reduce_sum x6 -> x1, other arithmetic: 17.2 us -> 0.96 us  [shards(): totals = jnp.sum(sums, axis=1)]
  transfers between devices with their start and end apart: 15 -> 0, of which waited for: 15 -> 0; matrix products, arithmetic and copies ran while one was open for 17% -> 0% of each run, Pallas kernels for 0% -> 0%
where the time goes in v1:
time: 431 us
  Pallas kernels  406 us (94%)
  local copies, waits for them, and re-layouts  13.2 us (3%)
  other arithmetic  9.79 us (2%)
    pallas_call x1, Pallas kernels, exchange(): pl.pallas_call(functools.partial(exchange_kernel, shard_count, tensor_cou...  406 us
    unnamed x26, local copies, waits for them, and re-layouts  12.7 us
    sub x3, other arithmetic, finish(): weights[position]  8.67 us

profile of v1, /device:TPU:0, one launch (start us, length us, event | category | flops | bytes accessed | tf_op | source)
XLA Modules:
  0.0 430.5 jit_solution(655324742511851053)
XLA Ops:
  0.6 406.1 %exchange.1 = (f32[4,256,512]{2,1,0:T(8,128)}, f32[2,256,1280]{2,1,0:T(8,128)}, f32[1,640,512]{2,1,0:T(8,128)}, f32[4,64,2048]{2,1,0:T(8,128)}, f32[2,160,2048]{...) custom-call(f32[4,256,512]{2,1,0:T(8,128)} %refs_0_.1, ...), custom_call_target="tpu_custom_call" | custom-call | tf_op jit(solution)/shard_map/exchange/pallas_call | solution.py:393
  406.8 0.0 copy-start
  406.8 1.0 reduce_sum.9
  407.8 0.1 add_divide_fusion
  407.9 0.0 copy-start.9
  407.9 0.6 slice.19
  409.1 3.1 multiply_subtract_fusion.2
  412.2 0.1 slice_multiply_fusion
  412.2 0.0 copy-done
  412.2 0.0 copy-start.1
  412.2 0.0 copy-start.4
  412.2 3.7 multiply_subtract_fusion
  416.0 0.0 copy-done.9
  416.0 0.0 copy-done.1
  416.0 0.0 copy-done.4
  416.0 0.0 copy-start.6
  416.0 1.9 multiply_subtract_fusion.1
  417.9 0.0 copy-done.6
  417.9 0.0 copy-start.3
  417.9 1.3 copy.28
  419.2 1.2 copy-done.3
  420.4 0.0 copy-start.8
  420.4 1.5 copy.29
  421.9 0.8 copy-done.8
  422.7 0.0 copy-start.5
  422.7 1.1 copy.30
  423.7 1.0 copy-done.5
  424.7 0.0 copy-start.2
  424.7 1.3 copy.31
  426.0 1.2 copy-done.2
  427.2 0.0 copy-start.7
  427.2 1.5 copy.32
  428.7 0.8 copy-done.7
  429.5 1.1 copy.33
  (1 shorter events, 0.0 us)
Async XLA Ops:
  406.8 5.4 %copy-start = (f32[2,256,1280]{2,1,0:T(8,128)S(1)}, f32[2,256,1280]{2,1,0:T(8,128)}, u32[]{:S(2)}) copy-start(f32[2,256,1280]{2,1,0:T(8,128)} %refs_1_.1) | copy-start | bytes 7864324
  407.9 8.1 %copy-start.9 = (f32[7]{0:T(128)}, f32[7]{0:T(128)S(1)}, u32[]{:S(2)}) copy-start(f32[7]{0:T(128)S(1)} %add_divide_fusion) | copy-start | bytes 88
  412.2 3.8 copy-start.1
  412.2 3.8 copy-start.4
  416.0 1.9 copy-start.6
  417.9 2.5 copy-start.3
  420.4 2.3 copy-start.8
  422.7 2.1 copy-start.5
  424.7 2.5 copy-start.2
  427.2 2.3 copy-start.7

commit v2 on v1

--- a/solution.py
+++ b/solution.py
@@ -8,8 +8,8 @@
 from jax.sharding import PartitionSpec as P
 
 MESH = pl.DeviceIdType.MESH
-RELAY_OUT = False
-RELAY_BACK = False
+RELAY_OUT = True
+RELAY_BACK = True
 
 beta_one = 0.9
 beta_two = 0.999

time: 431 us -> 342 us (0.79)
  Pallas kernels: 406 us -> 317 us
    pallas_call x1, Pallas kernels: 406 us -> 317 us  [exchange(): pl.pallas_call(functools.partial(exchange_kernel, shard_count, tensor_cou...]
where the time goes in v2:
time: 342 us; the launch traced here: 341 us
  Pallas kernels  317 us (93%)
  local copies, waits for them, and re-layouts  13.2 us (4%)
  other arithmetic  9.79 us (3%)
    pallas_call x1, Pallas kernels, exchange(): pl.pallas_call(functools.partial(exchange_kernel, shard_count, tensor_cou...  317 us
    unnamed x26, local copies, waits for them, and re-layouts  12.7 us
    sub x3, other arithmetic, finish(): weights[position]  8.67 us

profile of v2, /device:TPU:0, one launch (start us, length us, event | category | flops | bytes accessed | tf_op | source)
XLA Modules:
  0.0 341.3 jit_solution(15041390068999906905)
XLA Ops:
  0.6 316.9 %exchange.1 = (f32[4,256,512]{2,1,0:T(8,128)}, f32[2,256,1280]{2,1,0:T(8,128)}, f32[1,640,512]{2,1,0:T(8,128)}, f32[4,64,2048]{2,1,0:T(8,128)}, f32[2,160,2048]{...) custom-call(f32[4,256,512]{2,1,0:T(8,128)} %refs_0_.1, ...), custom_call_target="tpu_custom_call" | custom-call | tf_op jit(solution)/shard_map/exchange/pallas_call | solution.py:393
  317.6 0.0 copy-start
  317.6 1.0 reduce_sum.9
  318.5 0.1 add_divide_fusion
  318.6 0.0 copy-start.9
  318.6 0.6 slice.19
  319.9 3.1 multiply_subtract_fusion.2
  322.9 0.1 slice_multiply_fusion
  323.0 0.0 copy-done
  323.0 0.0 copy-start.1
  323.0 0.0 copy-start.4
  323.0 3.7 %multiply_subtract_fusion = f32[2,256,1280]{2,1,0:T(8,128)} fusion(f32[2,256,1280]{2,1,0:T(8,128)S(1)} %copy-done, f32[2,256,1280]{2,1,0:T(8,128)} %get-tuple-element.22, f32[2]{0:T(128)S(1)} %slice_multiply_fusion), kind=kLoop, calls=%fused_computation | loop fusion | flops 1310720 | bytes 7864328 | tf_op jit(solution)/shard_map/sub | solution.py:433
  326.8 0.0 copy-done.9
  326.8 0.0 copy-done.1
  326.8 0.0 copy-done.4
  326.8 0.0 copy-start.6
  326.8 1.9 multiply_subtract_fusion.1
  328.7 0.0 copy-done.6
  328.7 0.0 copy-start.3
  328.7 1.3 copy.28
  330.0 1.2 copy-done.3
  331.2 0.0 copy-start.8
  331.2 1.5 copy.29
  332.7 0.8 copy-done.8
  333.4 0.0 copy-start.5
  333.4 1.1 copy.30
  334.5 1.0 copy-done.5
  335.5 0.0 copy-start.2
  335.5 1.3 copy.31
  336.8 1.2 copy-done.2
  338.0 0.0 copy-start.7
  338.0 1.5 copy.32
  339.5 0.8 copy-done.7
  340.2 1.1 copy.33
  (1 shorter events, 0.0 us)
Async XLA Ops:
  317.6 5.4 %copy-start = (f32[2,256,1280]{2,1,0:T(8,128)S(1)}, f32[2,256,1280]{2,1,0:T(8,128)}, u32[]{:S(2)}) copy-start(f32[2,256,1280]{2,1,0:T(8,128)} %refs_1_.1) | copy-start | bytes 7864324
  318.6 8.1 %copy-start.9 = (f32[7]{0:T(128)}, f32[7]{0:T(128)S(1)}, u32[]{:S(2)}) copy-start(f32[7]{0:T(128)S(1)} %add_divide_fusion) | copy-start | bytes 88
  323.0 3.8 %copy-start.1 = (f32[4,256,512]{2,1,0:T(8,128)S(1)}, f32[4,256,512]{2,1,0:T(8,128)}, u32[]{:S(2)}) copy-start(f32[4,256,512]{2,1,0:T(8,128)} %refs_0_.1) | copy-start | bytes 6291460
  323.0 3.8 %copy-start.4 = (f32[4,256,512]{2,1,0:T(8,128)S(1)}, f32[4,256,512]{2,1,0:T(8,128)}, u32[]{:S(2)}) copy-start(f32[4,256,512]{2,1,0:T(8,128)} %get-tuple-element.21) | copy-start | bytes 6291460
  326.8 1.9 copy-start.6
  328.7 2.5 copy-start.3
  331.2 2.3 copy-start.8
  333.4 2.1 copy-start.5
  335.5 2.5 copy-start.2
  338.0 2.3 copy-start.7

commit v3 on v2

--- a/solution.py
+++ b/solution.py
@@ -8,7 +8,7 @@
 from jax.sharding import PartitionSpec as P
 
 MESH = pl.DeviceIdType.MESH
-RELAY_OUT = True
+RELAY_OUT = False
 RELAY_BACK = True
 
 beta_one = 0.9
@@ -318,13 +318,10 @@
         if position + 1 < count:
             forward_out(position + 1)
         moments(position)
-        if position >= 2:
-            forward_back(position - 2)
-    renew(0)
-    forward_back(count - 2)
-    renew(1)
-    forward_back(count - 1)
-    for position in range(2, count):
+    forward_back(0)
+    for position in range(count):
+        if position + 1 < count:
+            forward_back(position + 1)
         renew(position)
 
     def tell(step, carry):

time: 342 us -> 437 us (1.28)
  Pallas kernels: 317 us -> 412 us
    pallas_call x1, Pallas kernels: 317 us -> 412 us  [exchange(): pl.pallas_call(functools.partial(exchange_kernel, shard_count, tensor_cou...]
where the time goes in v3:
time: 437 us; the launch traced here: 436 us
  Pallas kernels  412 us (94%)
  local copies, waits for them, and re-layouts  13.2 us (3%)
  other arithmetic  9.79 us (2%)
    pallas_call x1, Pallas kernels, exchange(): pl.pallas_call(functools.partial(exchange_kernel, shard_count, tensor_cou...  412 us
    unnamed x26, local copies, waits for them, and re-layouts  12.7 us

profile of v3, /device:TPU:0, one launch (start us, length us, event | category | flops | bytes accessed | tf_op | source)
XLA Modules:
  0.0 436.3 jit_solution(12346955364751394189)
XLA Ops:
  0.6 411.9 %exchange.1 = (f32[4,256,512]{2,1,0:T(8,128)}, f32[2,256,1280]{2,1,0:T(8,128)}, f32[1,640,512]{2,1,0:T(8,128)}, f32[4,64,2048]{2,1,0:T(8,128)}, f32[2,160,2048]{...) custom-call(f32[4,256,512]{2,1,0:T(8,128)} %refs_0_.1, ...), custom_call_target="tpu_custom_call" | custom-call | tf_op jit(solution)/shard_map/exchange/pallas_call | solution.py:390
  412.5 0.0 copy-start
  412.6 1.0 reduce_sum.9
  413.5 0.1 add_divide_fusion
  413.6 0.0 copy-start.9
  413.6 0.6 slice.19
  414.9 3.1 multiply_subtract_fusion.2
  417.9 0.1 slice_multiply_fusion
  418.0 0.0 copy-done
  418.0 0.0 copy-start.1
  418.0 0.0 copy-start.4
  418.0 3.7 multiply_subtract_fusion
  421.7 0.0 copy-done.9
  421.7 0.0 copy-done.1
  421.7 0.0 copy-done.4
  421.8 0.0 copy-start.6
  421.8 1.9 multiply_subtract_fusion.1
  423.6 0.0 copy-done.6
  423.6 0.0 copy-start.3
  423.6 1.3 copy.28
  425.0 1.2 copy-done.3
  426.1 0.0 copy-start.8
  426.1 1.5 copy.29
  427.6 0.8 copy-done.8
  428.4 0.0 copy-start.5
  428.4 1.1 copy.30
  429.5 1.0 copy-done.5
  430.5 0.0 copy-start.2
  430.5 1.3 copy.31
  431.8 1.2 copy-done.2
  433.0 0.0 copy-start.7
  433.0 1.5 copy.32
  434.5 0.8 copy-done.7
  435.2 1.1 copy.33
  (1 shorter events, 0.0 us)
Async XLA Ops:
  412.5 5.4 %copy-start = (f32[2,256,1280]{2,1,0:T(8,128)S(1)}, f32[2,256,1280]{2,1,0:T(8,128)}, u32[]{:S(2)}) copy-start(f32[2,256,1280]{2,1,0:T(8,128)} %refs_1_.1) | copy-start | bytes 7864324
  413.6 8.1 %copy-start.9 = (f32[7]{0:T(128)}, f32[7]{0:T(128)S(1)}, u32[]{:S(2)}) copy-start(f32[7]{0:T(128)S(1)} %add_divide_fusion) | copy-start | bytes 88
  418.0 3.8 copy-start.1
  418.0 3.8 copy-start.4
  421.8 1.9 copy-start.6
  423.6 2.5 copy-start.3
  426.1 2.3 copy-start.8
  428.4 2.1 copy-start.5
  430.5 2.5 copy-start.2
  433.0 2.3 copy-start.7

commit v4 on v3

--- a/solution.py
+++ b/solution.py
@@ -8,8 +8,8 @@
 from jax.sharding import PartitionSpec as P
 
 MESH = pl.DeviceIdType.MESH
-RELAY_OUT = False
-RELAY_BACK = True
+RELAY_OUT = True
+RELAY_BACK = False
 
 beta_one = 0.9
 beta_two = 0.999

time: 437 us -> 334 us (0.76)
  Pallas kernels: 412 us -> 309 us
    pallas_call x1, Pallas kernels: 412 us -> 309 us  [exchange(): pl.pallas_call(functools.partial(exchange_kernel, shard_count, tensor_cou...]
where the time goes in v4:
time: 334 us
  Pallas kernels  309 us (93%)
  local copies, waits for them, and re-layouts  13.2 us (4%)
  other arithmetic  9.79 us (3%)
    pallas_call x1, Pallas kernels, exchange(): pl.pallas_call(functools.partial(exchange_kernel, shard_count, tensor_cou...  309 us
    unnamed x26, local copies, waits for them, and re-layouts  12.7 us
    sub x3, other arithmetic, finish(): weights[position]  8.67 us

profile of v4, /device:TPU:0, one launch (start us, length us, event | category | flops | bytes accessed | tf_op | source)
XLA Modules:
  0.0 333.7 jit_solution(749797848440989491)
XLA Ops:
  0.6 309.3 %exchange.1 = (f32[4,256,512]{2,1,0:T(8,128)}, f32[2,256,1280]{2,1,0:T(8,128)}, f32[1,640,512]{2,1,0:T(8,128)}, f32[4,64,2048]{2,1,0:T(8,128)}, f32[2,160,2048]{...) custom-call(f32[4,256,512]{2,1,0:T(8,128)} %refs_0_.1, ...), custom_call_target="tpu_custom_call" | custom-call | tf_op jit(solution)/shard_map/exchange/pallas_call | solution.py:390
  310.0 0.0 copy-start
  310.0 1.0 reduce_sum.9
  311.0 0.1 add_divide_fusion
  311.0 0.0 copy-start.9
  311.0 0.6 slice.19
  312.3 3.1 multiply_subtract_fusion.2
  315.4 0.1 slice_multiply_fusion
  315.4 0.0 copy-done
  315.4 0.0 copy-start.1
  315.4 0.0 copy-start.4
  315.4 3.7 %multiply_subtract_fusion = f32[2,256,1280]{2,1,0:T(8,128)} fusion(f32[2,256,1280]{2,1,0:T(8,128)S(1)} %copy-done, f32[2,256,1280]{2,1,0:T(8,128)} %get-tuple-element.22, f32[2]{0:T(128)S(1)} %slice_multiply_fusion), kind=kLoop, calls=%fused_computation | loop fusion | flops 1310720 | bytes 7864328 | tf_op jit(solution)/shard_map/sub | solution.py:430
  319.2 0.0 copy-done.9
  319.2 0.0 copy-done.1
  319.2 0.0 copy-done.4
  319.2 0.0 copy-start.6
  319.2 1.9 multiply_subtract_fusion.1
  321.1 0.0 copy-done.6
  321.1 0.0 copy-start.3
  321.1 1.3 copy.28
  322.4 1.2 copy-done.3
  323.6 0.0 copy-start.8
  323.6 1.5 copy.29
  325.1 0.8 copy-done.8
  325.8 0.0 copy-start.5
  325.8 1.1 copy.30
  326.9 1.0 copy-done.5
  327.9 0.0 copy-start.2
  327.9 1.3 copy.31
  329.2 1.2 copy-done.2
  330.4 0.0 copy-start.7
  330.4 1.5 copy.32
  331.9 0.8 copy-done.7
  332.7 1.1 copy.33
  (1 shorter events, 0.0 us)
Async XLA Ops:
  310.0 5.4 %copy-start = (f32[2,256,1280]{2,1,0:T(8,128)S(1)}, f32[2,256,1280]{2,1,0:T(8,128)}, u32[]{:S(2)}) copy-start(f32[2,256,1280]{2,1,0:T(8,128)} %refs_1_.1) | copy-start | bytes 7864324
  311.0 8.1 %copy-start.9 = (f32[7]{0:T(128)}, f32[7]{0:T(128)S(1)}, u32[]{:S(2)}) copy-start(f32[7]{0:T(128)S(1)} %add_divide_fusion) | copy-start | bytes 88
  315.4 3.8 %copy-start.1 = (f32[4,256,512]{2,1,0:T(8,128)S(1)}, f32[4,256,512]{2,1,0:T(8,128)}, u32[]{:S(2)}) copy-start(f32[4,256,512]{2,1,0:T(8,128)} %refs_0_.1) | copy-start | bytes 6291460
  315.4 3.8 %copy-start.4 = (f32[4,256,512]{2,1,0:T(8,128)S(1)}, f32[4,256,512]{2,1,0:T(8,128)}, u32[]{:S(2)}) copy-start(f32[4,256,512]{2,1,0:T(8,128)} %get-tuple-element.21) | copy-start | bytes 6291460
  319.2 1.9 copy-start.6
  321.1 2.5 copy-start.3
  323.6 2.3 copy-start.8
  325.8 2.1 copy-start.5
  327.9 2.5 copy-start.2
  330.4 2.3 copy-start.7

commit v5 on v4

--- a/solution.py
+++ b/solution.py
@@ -8,8 +8,6 @@
 from jax.sharding import PartitionSpec as P
 
 MESH = pl.DeviceIdType.MESH
-RELAY_OUT = True
-RELAY_BACK = False
 
 beta_one = 0.9
 beta_two = 0.999
@@ -57,7 +55,7 @@
     return jnp.swapaxes(spread, 1, 2)
 
 
-ORDER = ((1, 0), (1, 1), (2, 0), (0, 0), (0, 1), (0, 2), (0, 3))
+ORDER = ((0, 0), (1, 0), (1, 1), (2, 0), (0, 1), (0, 2), (0, 3))
 
 
 def row_of(array, index):
@@ -69,12 +67,12 @@
     updates, firsts_new, seconds_new, sums_out = refs[12:15], refs[15:18], refs[18:21], refs[21]
     grad_v, turned_v, flat_v, back_v = refs[22:25], refs[25:28], refs[28:31], refs[31:34]
     first_v, second_v, weight_v = refs[34:37], refs[37:40], refs[40:43]
-    out_stop, back_stop = refs[43:46], refs[46:49]
-    partial, sums_v = refs[49], refs[50]
+    out_stop = refs[43:46]
+    partial, sums_v = refs[46], refs[47]
     (
         load_g, load_m, load_v, load_w, out_send, out_recv, stop_recv, stop_send,
-        back_send, back_recv, bstop_recv, bstop_send, save_u, save_m, save_v, total_sem,
-    ) = refs[51:67]
+        back_send, back_recv, save_u, save_m, save_v, total_sem,
+    ) = refs[48:62]
 
     groups = shard_count // tensor_count
     half = tensor_count // 2
@@ -85,8 +83,7 @@
     side = t // half
     home = s // groups
     mine = lax.rem(s, groups) * tensor_count + t
-    my_slot = lax.rem(s, groups) * half + lax.rem(t, half)
-    same_side = home // half == side
+    turn_from = s + lax.rem(t, half) * (shard_count // half)
 
     for position, (a, i) in enumerate(ORDER):
         pltpu.make_async_copy(grads[a].at[i], grad_v[a].at[i], load_g.at[position]).start()
@@ -143,54 +140,42 @@
 
         lax.fori_loop(0, col_block // 128, one, 0)
 
+    def send_mate(position):
+        a, i = ORDER[position]
+        row_block, col_block, col_flat = sizes(a)
+        other_side = mate // half
+        for y in range(groups):
+            rows = pl.ds(
+                pl.multiple_of((y * tensor_count + other_side * half) * col_flat, 8),
+                half * col_flat,
+            )
+            remote(
+                turned_v[a].at[i, rows, :],
+                out_stop[a].at[i, pl.ds(y * half * col_flat, half * col_flat), :],
+                out_send.at[position],
+                stop_recv.at[position],
+                (s, mate),
+            ).start()
+
     def send_out(position):
         a, i = ORDER[position]
         row_block, col_block, col_flat = sizes(a)
         land = pl.ds(pl.multiple_of(s * row_block, 128), row_block)
-        send, recv = out_send.at[position], out_recv.at[position]
-        if RELAY_OUT:
-            other_side = mate // half
-            for y in range(groups):
-                rows = pl.ds(
-                    pl.multiple_of((y * tensor_count + other_side * half) * col_flat, 8),
-                    half * col_flat,
-                )
-                remote(
-                    turned_v[a].at[i, rows, :],
-                    out_stop[a].at[i, pl.ds(y * half * col_flat, half * col_flat), :],
-                    send,
-                    stop_recv.at[position],
-                    (s, mate),
-                ).start()
-            for y in range(groups):
-                for core in range(half):
-                    target = side * half + core
-                    k = y * tensor_count + target
-                    rows = pl.ds(pl.multiple_of(k * col_flat, 8), col_flat)
-                    shard_to = groups * t + y
-                    send_or_keep(
-                        jnp.logical_and(shard_to == s, target == t),
-                        turned_v[a].at[i, rows, :],
-                        flat_v[a].at[i, :, land],
-                        send,
-                        recv,
-                        (shard_to, target),
-                    )
-        else:
-            for k in range(shard_count):
-                shard_to, target = groups * t + k // tensor_count, k % tensor_count
+        for y in range(groups):
+            for core in range(half):
+                target = side * half + core
+                k = y * tensor_count + target
+                shard_to = groups * t + y
                 send_or_keep(
                     jnp.logical_and(shard_to == s, target == t),
-                    turned_v[a].at[i, pl.ds(k * col_flat, col_flat), :],
+                    turned_v[a].at[i, pl.ds(pl.multiple_of(k * col_flat, 8), col_flat), :],
                     flat_v[a].at[i, :, land],
-                    send,
-                    recv,
+                    out_send.at[position],
+                    out_recv.at[position],
                     (shard_to, target),
                 )
 
     def forward_out(position):
-        if not RELAY_OUT:
-            return
         a, i = ORDER[position]
         row_block, col_block, col_flat = sizes(a)
         wait_bytes(out_stop[a].at[i], stop_recv.at[position])
@@ -231,56 +216,18 @@
 
         lax.fori_loop(0, col_flat // 8, one, 0)
         rows = pl.ds(pl.multiple_of(mine * col_flat, 8), col_flat)
-        slot = pl.ds(pl.multiple_of(my_slot * col_flat, 8), col_flat)
-        for shard_to in range(shard_count):
-            piece = flat_v[a].at[i, :, pl.ds(shard_to * row_block, row_block)]
-
-            def direct():
-                send_or_keep(
-                    jnp.logical_and(s == shard_to, home == t),
-                    piece,
-                    back_v[a].at[i, rows, :],
-                    back_send.at[position],
-                    back_recv.at[position],
-                    (shard_to, home),
-                )
-
-            def by_stop():
-                stop = lax.rem(home + half, tensor_count)
-                send_or_keep(
-                    jnp.logical_and(s == shard_to, stop == t),
-                    piece,
-                    back_stop[a].at[i, slot, :],
-                    back_send.at[position],
-                    bstop_recv.at[position],
-                    (shard_to, stop),
-                )
-
-            if RELAY_BACK:
-                pl.when(same_side)(direct)
-                pl.when(jnp.logical_not(same_side))(by_stop)
-            else:
-                direct()
+        for step in range(shard_count):
+            shard_to = lax.rem(turn_from + step, shard_count)
+            send_or_keep(
+                jnp.logical_and(s == shard_to, home == t),
+                flat_v[a].at[i, :, pl.ds(pl.multiple_of(shard_to * row_block, 128), row_block)],
+                back_v[a].at[i, rows, :],
+                back_send.at[position],
+                back_recv.at[position],
+                (shard_to, home),
+            )
         pltpu.make_async_copy(first_v[a].at[i], firsts_new[a].at[i], save_m.at[position]).start()
         pltpu.make_async_copy(second_v[a].at[i], seconds_new[a].at[i], save_v.at[position]).start()
-
-    def forward_back(position):
-        if not RELAY_BACK:
-            return
-        a, i = ORDER[position]
-        row_block, col_block, col_flat = sizes(a)
-        wait_bytes(back_stop[a].at[i], bstop_recv.at[position])
-        for y in range(groups):
-            rows = pl.ds(
-                pl.multiple_of((y * tensor_count + side * half) * col_flat, 8), half * col_flat
-            )
-            remote(
-                back_stop[a].at[i, pl.ds(y * half * col_flat, half * col_flat), :],
-                back_v[a].at[i, rows, :],
-                bstop_send.at[position],
-                back_recv.at[position],
-                (s, mate),
-            ).start()
 
     def renew(position):
         a, i = ORDER[position]
@@ -309,19 +256,20 @@
     partial[me, :, :] = jnp.zeros((16, 128), jnp.float32)
     turn(0)
     pl.semaphore_wait(barrier, devices - 1)
+    send_mate(0)
+    turn(1)
+    send_mate(1)
     send_out(0)
-    for position in range(1, count):
-        turn(position)
-        send_out(position)
-    forward_out(0)
     for position in range(count):
+        forward_out(position)
+        if position + 2 < count:
+            turn(position + 2)
+            send_mate(position + 2)
         if position + 1 < count:
-            forward_out(position + 1)
+            send_out(position + 1)
+    for position in range(count):
         moments(position)
-    forward_back(0)
     for position in range(count):
-        if position + 1 < count:
-            forward_back(position + 1)
         renew(position)
 
     def tell(step, carry):
@@ -344,11 +292,7 @@
     pltpu.make_async_copy(sums_v, sums_out, total_sem.at[2]).start()
     wait_bytes(partial.at[pl.ds(0, devices - 1)], total_sem.at[0])
 
-    out_self = home == t if RELAY_OUT else home == t
-    stop_self = home == mate
-    back_self = home == t
-    if RELAY_BACK:
-        back_self = jnp.logical_or(home == t, lax.rem(home + half, tensor_count) == t)
+    to_self, stop_self = home == t, home == mate
 
     def wait_less(is_less, ref, i, total_rows, piece_rows, sem):
         @pl.when(is_less)
@@ -361,12 +305,9 @@
 
     for position, (a, i) in enumerate(ORDER):
         row_block, col_block, col_flat = sizes(a)
-        wait_less(out_self, turned_v[a], i, col_block, col_flat, out_send.at[position])
-        wait_less(back_self, turned_v[a], i, col_block, col_flat, back_send.at[position])
-        if RELAY_OUT:
-            wait_less(stop_self, out_stop[a], i, col_block // 2, col_flat, stop_send.at[position])
-        if RELAY_BACK:
-            wait_bytes(back_stop[a].at[i], bstop_send.at[position])
+        wait_less(to_self, turned_v[a], i, col_block, col_flat, out_send.at[position])
+        wait_less(to_self, turned_v[a], i, col_block, col_flat, back_send.at[position])
+        wait_less(stop_self, out_stop[a], i, col_block // 2, col_flat, stop_send.at[position])
         wait_bytes(grad_v[a].at[i], save_u.at[position])
         wait_bytes(first_v[a].at[i], save_m.at[position])
         wait_bytes(second_v[a].at[i], save_v.at[position])
@@ -382,10 +323,10 @@
     devices = shard_count * tensor_count
     shapes = blocks + flats + flats + [(16, 128)]
     scratch = []
-    for group in (blocks, turned, flats, turned, flats, flats, blocks, halves, halves):
+    for group in (blocks, turned, flats, turned, flats, flats, blocks, halves):
         scratch += [pltpu.VMEM(shape, f32) for shape in group]
     scratch += [pltpu.VMEM((devices, 16, 128), f32), pltpu.VMEM((16, 128), f32)]
-    scratch += [pltpu.SemaphoreType.DMA((len(ORDER),))] * 15 + [pltpu.SemaphoreType.DMA((3,))]
+    scratch += [pltpu.SemaphoreType.DMA((len(ORDER),))] * 13 + [pltpu.SemaphoreType.DMA((3,))]
     anywhere = pl.BlockSpec(memory_space=pl.ANY)
     return pl.pallas_call(
         functools.partial(exchange_kernel, shard_count, tensor_count),
@@ -400,6 +341,67 @@
     )(*weights, *grads, *firsts, *seconds)
 
 
+def step_kernel(*refs):
+    weights, updates, firsts, seconds, sums = refs[0:3], refs[3:6], refs[6:9], refs[9:12], refs[12]
+    weights_new, firsts_new, seconds_new, trust = refs[13:16], refs[16:19], refs[19:22], refs[22]
+    weight_v, update_v, first_v, second_v = refs[23:26], refs[26:29], refs[29:32], refs[32:35]
+    load_w, load_u, load_m, load_v, save_w, save_m, save_v = refs[35:42]
+    for position, (a, i) in enumerate(ORDER):
+        pltpu.make_async_copy(updates[a].at[i], update_v[a].at[i], load_u.at[position]).start()
+        pltpu.make_async_copy(weights[a].at[i], weight_v[a].at[i], load_w.at[position]).start()
+        pltpu.make_async_copy(firsts[a].at[i], first_v[a].at[i], load_m.at[position]).start()
+        pltpu.make_async_copy(seconds[a].at[i], second_v[a].at[i], load_v.at[position]).start()
+    totals = jnp.sum(sums[...], axis=1, keepdims=True)
+    ratio = jnp.sqrt(totals[0:8]) / (jnp.sqrt(totals[8:16]) + epsilon)
+    trust[...] = jnp.broadcast_to(ratio, (8, 128))
+
+    def wait_bytes(ref, sem):
+        pltpu.make_async_copy(ref, ref, sem).wait()
+
+    for position, (a, i) in enumerate(ORDER):
+        row = row_of(a, i)
+        scale = learn_rate * trust[row : row + 1, 0:1]
+        wait_bytes(update_v[a].at[i], load_u.at[position])
+        wait_bytes(weight_v[a].at[i], load_w.at[position])
+
+        def one(j, carry):
+            rows = pl.ds(pl.multiple_of(j * 8, 8), 8)
+            weight_v[a][i, rows, :] = weight_v[a][i, rows, :] - scale * update_v[a][i, rows, :]
+            return carry
+
+        lax.fori_loop(0, weights[a].shape[1] // 8, one, 0)
+        pltpu.make_async_copy(weight_v[a].at[i], weights_new[a].at[i], save_w.at[position]).start()
+        wait_bytes(first_v[a].at[i], load_m.at[position])
+        pltpu.make_async_copy(first_v[a].at[i], firsts_new[a].at[i], save_m.at[position]).start()
+        wait_bytes(second_v[a].at[i], load_v.at[position])
+        pltpu.make_async_copy(second_v[a].at[i], seconds_new[a].at[i], save_v.at[position]).start()
+    for position, (a, i) in enumerate(ORDER):
+        wait_bytes(weight_v[a].at[i], save_w.at[position])
+        wait_bytes(first_v[a].at[i], save_m.at[position])
+        wait_bytes(second_v[a].at[i], save_v.at[position])
+
+
+def apply_step(weights, updates, firsts, seconds, sums):
+    f32 = jnp.float32
+    blocks = [matrix.shape for matrix in weights]
+    flats = [matrix.shape for matrix in firsts]
+    anywhere = pl.BlockSpec(memory_space=pl.ANY)
+    whole = pl.BlockSpec(memory_space=pltpu.VMEM)
+    scratch = [pltpu.VMEM(shape, f32) for shape in blocks + blocks + flats + flats]
+    scratch += [pltpu.SemaphoreType.DMA((len(ORDER),))] * 7
+    return pl.pallas_call(
+        step_kernel,
+        out_shape=[
+            jax.ShapeDtypeStruct(shape, f32) for shape in blocks + flats + flats + [(8, 128)]
+        ],
+        in_specs=[anywhere] * 12 + [whole],
+        out_specs=[anywhere] * 9 + [whole],
+        scratch_shapes=scratch,
+        compiler_params=pltpu.CompilerParams(vmem_limit_bytes=48 * 1024 * 1024),
+        name="apply_step",
+    )(*weights, *updates, *firsts, *seconds, sums)
+
+
 def fits(weights, firsts, shard_count, tensor_count):
     if shard_count % tensor_count or tensor_count % 2:
         return False
@@ -419,9 +421,8 @@
         return plain(weights, grads, firsts, seconds, shard_count, tensor_count)
     out = exchange(weights, grads, firsts, seconds, shard_count, tensor_count)
     updates, firsts_new, seconds_new, sums = out[0:3], out[3:6], out[6:9], out[9]
-    totals = jnp.sum(sums, axis=1)
-    trust_ratio = jnp.sqrt(totals[0:7]) / (jnp.sqrt(totals[8:15]) + epsilon)
-    return finish(weights, updates, firsts_new, seconds_new, trust_ratio)
+    done = apply_step(weights, updates, firsts_new, seconds_new, sums)
+    return (*done[0:9], done[9][0:7, 0])
 
 
 def finish(weights, updates, firsts_new, seconds_new, trust_ratio):

time: 334 us -> 308 us (0.922)
  other arithmetic: 9.79 us -> 0 us
  local copies, waits for them, and re-layouts: 13.2 us -> 5.27 us
  Pallas kernels: 309 us -> 302 us
    pallas_call x1, Pallas kernels: 309 us -> 287 us  [exchange(): pl.pallas_call(functools.partial(exchange_kernel, shard_count, tensor_cou...]
    pallas_call x0 -> x1, Pallas kernels: none -> 14.7 us  [apply_step(): pl.pallas_call(step_kernel, out_shape=[jax.ShapeDtypeStruct(shape, f32) f...]
    sub x3 -> x0, other arithmetic: 8.67 us -> none  [finish(): weights[position]]
    unnamed x26 -> x10, local copies, waits for them, and re-layouts: 12.7 us -> 4.64 us
where the time goes in v5:
time: 308 us
  Pallas kernels  302 us (98%)
  local copies, waits for them, and re-layouts  5.27 us (2%)
    pallas_call x1, Pallas kernels, exchange(): pl.pallas_call(functools.partial(exchange_kernel, shard_count, tensor_cou...  287 us
    pallas_call x1, Pallas kernels, apply_step(): pl.pallas_call(step_kernel, out_shape=[jax.ShapeDtypeStruct(shape, f32) f...  14.7 us

profile of v5, /device:TPU:0, one launch (start us, length us, event | category | flops | bytes accessed | tf_op | source)
XLA Modules:
  0.0 308.0 jit_solution(3411741671787943334)
XLA Ops:
  0.6 0.0 copy-start
  0.7 287.4 %exchange.1 = (f32[4,256,512]{2,1,0:T(8,128)}, f32[2,256,1280]{2,1,0:T(8,128)}, f32[1,640,512]{2,1,0:T(8,128)}, f32[4,64,2048]{2,1,0:T(8,128)}, f32[2,160,2048]{...) custom-call(f32[4,256,512]{2,1,0:T(8,128)} %refs_0_.3, ...), custom_call_target="tpu_custom_call" | custom-call | tf_op jit(solution)/shard_map/exchange/pallas_call | solution.py:331
  288.0 0.0 copy-done
  288.0 0.0 copy-start.1
  288.0 1.3 copy-done.1
  289.3 0.0 copy-start.2
  289.3 1.3 copy-done.2
  290.7 0.0 copy-start.3
  290.7 1.3 copy-done.3
  292.0 0.0 copy-start.4
  292.0 0.7 copy-done.4
  292.7 14.7 %apply_step.1 = (f32[4,256,512]{2,1,0:T(8,128)}, f32[2,256,1280]{2,1,0:T(8,128)}, f32[1,640,512]{2,1,0:T(8,128)}, f32[4,64,2048]{2,1,0:T(8,128)}, f32[2,160,2048...) custom-call(f32[4,256,512]{2,1,0:T(8,128)} %refs_0_.3, ...), custom_call_target="tpu_custom_call" | custom-call | tf_op jit(solution)/shard_map/apply_step/pallas_call | solution.py:392
  307.4 0.6 slice_reduce_fusion
Async XLA Ops:
  0.6 287.4 %copy-start = (f32[1,640,512]{2,1,0:T(8,128)S(1)}, f32[1,640,512]{2,1,0:T(8,128)}, u32[]{:S(2)}) copy-start(f32[1,640,512]{2,1,0:T(8,128)} %refs_2_.3) | copy-start | bytes 3932164
  288.0 1.3 copy-start.1
  289.3 1.3 copy-start.2
  290.7 1.3 copy-start.3
  292.0 0.7 copy-start.4
